TPU v7x, 512 devices: a whole 4x4x16 slice. The times are simulated.
512 devices in a mesh: depth: 8 (over z_hi, core), lat: 64 (over x, z_lo, y).
Axes of the slice: x: 4, y: 4, z: 16 (z_hi: 4, z_lo: 4; z = z_hi * 4 + z_lo), core: 2. Of those that a mesh axis runs over, the one named last changes fastest.
Arguments:
- fields: float32 [6, 384, 64, 512], P(None, 'lat', 'depth'), may hold values from -3 to 3
- material: int32 [384, 64, 512], P('lat', 'depth'), may hold values from 0 to 3
- source_mask: int32 [384, 64, 512], P('lat', 'depth'), may hold values 0 or 1
- eps_table: float32 [4], replicated, may hold values from 1 to 6
- kerr_table: float32 [4], replicated, may hold values from 0.3 to 3
Outputs:
- fields_out: float32 [6, 384, 64, 512], P(None, 'lat', 'depth')
- image: float32 [384, 8, 512], P('lat', None, 'depth')
Inputs may be any that keep to these rules, and one draw needn't show every extreme that they name: material indexes the tables.
All inputs are finite; a program needn't handle non-finite values. No bound on the sum of `source_mask` on one device may be relied on, other than what follows from the above.
Results may differ from a plain program's by a relative error of at most 0.0003.
Values sent between devices are 32-bit elements; how exact they have to be, the bound alone decides.
A program may use at most 64 MiB of HBM per device.

v0:
```python
import math
import jax
import jax.numpy as jnp
from jax import lax
from jax.sharding import PartitionSpec as P

STEPS = 16
COURANT = 0.55
OMEGAS = (0.9, 1.3)
SOURCE_AMP = 1.0
QUARTERS = (3, 5)
HIGHEST = lax.Precision.HIGHEST


def padded_2(block, sides, width):
    for axis, dim in sides:
        count = lax.axis_size(axis)
        forward = [(i, i + 1) for i in range(count - 1)]
        backward = [(target, source) for source, target in forward]
        low = lax.ppermute(
            lax.slice_in_dim(block, block.shape[dim] - width, None, axis=dim), axis, forward
        )
        high = lax.ppermute(lax.slice_in_dim(block, 0, width, axis=dim), axis, backward)
        block = jnp.concatenate([low, block, high], axis=dim)
    return block


def from_root(block, axis, owner):
    block = jnp.where(lax.axis_index(axis) == owner, block, jnp.zeros_like(block))
    return lax.psum(block, axis)


def forward_diff(field, along):
    length = field.shape[along]
    ahead = lax.slice_in_dim(field, 1, length, axis=along)
    ahead = jnp.concatenate(
        [ahead, jnp.zeros_like(lax.slice_in_dim(field, 0, 1, axis=along))], axis=along
    )
    return ahead - field


def backward_diff(field, along):
    length = field.shape[along]
    behind = lax.slice_in_dim(field, 0, length - 1, axis=along)
    behind = jnp.concatenate(
        [jnp.zeros_like(lax.slice_in_dim(field, 0, 1, axis=along)), behind], axis=along
    )
    return field - behind


def drive(moment):
    middle = moment + 0.5
    return SOURCE_AMP * (jnp.sin(OMEGAS[0] * middle) + jnp.sin(OMEGAS[1] * middle))


def yee_step(fields, permittivity, kerr_coef, source_flag, inside, pulse):
    elec_x, elec_y, elec_z = (fields[0], fields[1], fields[2])
    magn_x, magn_y, magn_z = (fields[3], fields[4], fields[5])
    magn_x = (magn_x - COURANT * (forward_diff(elec_z, 2) - forward_diff(elec_y, 1))) * inside
    magn_y = (magn_y - COURANT * (forward_diff(elec_x, 1) - forward_diff(elec_z, 0))) * inside
    magn_z = (magn_z - COURANT * (forward_diff(elec_y, 0) - forward_diff(elec_x, 2))) * inside
    energy = elec_x * elec_x + elec_y * elec_y + elec_z * elec_z
    factor = COURANT / (permittivity + kerr_coef * energy)
    new_x = (
        elec_x
        + factor * (backward_diff(magn_z, 2) - backward_diff(magn_y, 1))
        + source_flag * pulse
    ) * inside
    new_y = (elec_y + factor * (backward_diff(magn_x, 1) - backward_diff(magn_z, 0))) * inside
    new_z = (elec_z + factor * (backward_diff(magn_y, 0) - backward_diff(magn_x, 2))) * inside
    return jnp.stack([new_x, new_y, new_z, magn_x, magn_y, magn_z])


def lookup(material, table):
    result = jnp.zeros(material.shape, jnp.float32)
    for level in range(table.shape[0]):
        result = jnp.where(material == level, table[level], result)
    return result


def accumulate(spectrum, plane, moment):
    later = moment + 1.0
    trig = jnp.stack(
        [jnp.stack([jnp.cos(omega * later), -jnp.sin(omega * later)]) for omega in OMEGAS]
    )
    return spectrum + trig[:, None, :, None, None] * plane[None, :, None, :, :]


def chirp(row_index, col_index, length):
    gap = row_index[:, None] - col_index[None, :]
    squared = gap * gap
    reals, imags = ([], [])
    for quarter in QUARTERS:
        wrapped = quarter * squared % (8 * length)
        phase = wrapped.astype(jnp.float32) * (math.pi / (4.0 * length))
        reals.append(jnp.cos(phase) / math.sqrt(length))
        imags.append(jnp.sin(phase) / math.sqrt(length))
    return (jnp.stack(reals), jnp.stack(imags))


def column_transform(real, imag, y_real, y_imag):
    v_real = jnp.einsum("fcxy,fyk->fcxk", real, y_real, precision=HIGHEST) - jnp.einsum(
        "fcxy,fyk->fcxk", imag, y_imag, precision=HIGHEST
    )
    v_imag = jnp.einsum("fcxy,fyk->fcxk", real, y_imag, precision=HIGHEST) + jnp.einsum(
        "fcxy,fyk->fcxk", imag, y_real, precision=HIGHEST
    )
    return (v_real, v_imag)


def row_transform(x_real, x_imag, v_real, v_imag):
    w_real = jnp.einsum("fix,fcxk->ifck", x_real, v_real, precision=HIGHEST) - jnp.einsum(
        "fix,fcxk->ifck", x_imag, v_imag, precision=HIGHEST
    )
    w_imag = jnp.einsum("fix,fcxk->ifck", x_real, v_imag, precision=HIGHEST) + jnp.einsum(
        "fix,fcxk->ifck", x_imag, v_real, precision=HIGHEST
    )
    return jnp.stack([w_real, w_imag], axis=3)


def local(fields, material, source_mask, eps_table, kerr_table):
    width_x = fields.shape[1]
    depth_z = fields.shape[2]
    span_y = fields.shape[3]
    lat_count = lax.axis_size("lat")
    depth_count = lax.axis_size("depth")
    total_x = width_x * lat_count
    total_z = depth_z * depth_count
    lat_pos = lax.axis_index("lat")
    depth_pos = lax.axis_index("depth")
    coefs = jnp.stack(
        [lookup(material, eps_table), lookup(material, kerr_table), source_mask.astype(jnp.float32)]
    )
    empty_spectrum = jnp.zeros((2, 2, 2, width_x, span_y), jnp.float32)
    rim_width = ((0, 0), (1, 1), (1, 1), (0, 0))
    eps_pad = jnp.pad(coefs[0:1], rim_width, constant_values=1.0)
    rest_pad = jnp.pad(coefs[1:3], rim_width, constant_values=0.0)
    sub = jnp.concatenate([eps_pad, rest_pad], axis=0)
    place_x = lat_pos * width_x - 1 + jnp.arange(width_x + 2 * 1, dtype=jnp.int32)
    place_z = depth_pos * depth_z - 1 + jnp.arange(depth_z + 2 * 1, dtype=jnp.int32)
    valid_x = (place_x >= 0) & (place_x < total_x)
    valid_z = (place_z >= 0) & (place_z < total_z)
    valid = valid_x[:, None] & valid_z[None, :]
    setup_inside = valid.astype(jnp.float32)[:, :, None]
    setup_permittivity = jnp.where(valid[:, :, None], sub[0], 1.0)
    kerr_coef = sub[1]
    source_flag = sub[2]

    def one_step(step, carry):
        state, spectrum = carry
        padded = padded_2(state, (("depth", 2), ("lat", 1)), 1)
        moment = step.astype(jnp.float32)
        padded = yee_step(
            padded, setup_permittivity, kerr_coef, source_flag, setup_inside, drive(moment)
        )
        state = padded[:, 1:-1, 1:-1]
        spectrum = accumulate(spectrum, state[0:2, :, depth_z - 1, :], moment)
        return (state, spectrum)

    state, spectrum = lax.fori_loop(0, STEPS, one_step, (fields, empty_spectrum))
    spectrum = from_root(spectrum, "depth", depth_count - 1)
    col_count = span_y // depth_count
    col_index = depth_pos * col_count + jnp.arange(col_count, dtype=jnp.int32)
    y_real, y_imag = chirp(jnp.arange(span_y, dtype=jnp.int32), col_index, span_y)
    v_real, v_imag = column_transform(spectrum[:, :, 0], spectrum[:, :, 1], y_real, y_imag)
    row_local = lat_pos * width_x + jnp.arange(width_x, dtype=jnp.int32)
    row_index = jnp.arange(width_x * lax.axis_size("lat"), dtype=jnp.int32)
    x_real, x_imag = chirp(row_index, row_local, total_x)
    image = lax.psum_scatter(
        row_transform(x_real, x_imag, v_real, v_imag), "lat", scatter_dimension=0, tiled=True
    )
    return (state, image.reshape(width_x, 8, col_count))


def solution(mesh):
    placed = (
        P(None, "lat", "depth", None),
        P("lat", "depth", None),
        P("lat", "depth", None),
        P(),
        P(),
    )
    return jax.shard_map(
        local,
        mesh=mesh,
        in_specs=placed,
        out_specs=(P(None, "lat", "depth", None), P("lat", None, "depth")),
        check_vma=False,
    )
```

profile of v0, /device:TPU:8, one launch (start us, length us, event | category | flops | bytes accessed | tf_op | source)
XLA Modules:
  0.0 1378.4 jit_solution(10861475274174279404)
XLA Ops:
  11.0 5.2 select_bitcast_fusion
  17.2 478.5 %while.16 = (s32[]{:T(128)}, f32[6,6,8,512]{3,0,1,2:T(8,128)S(1)}, f32[2,2,2,6,512]{4,3,2,1,0:T(8,128)S(1)}, f32[8,10,512]{2,0,1:T(8,128)S(1)}, f32[8,10,512]{2,...) while((s32[]{:T(128)}, f32[6,6,8,512]{3,0,1,2:T(8,128)S(1)}, ...), condition=%wide.region_1.2_spmd.clone, body=%wide.region_0.1_spmd.clone.sunk | while | flops 2527413 | bytes 23437268 | solution.py:160
  21.4 8.1 collective-permute-done.1
  45.5 7.6 collective-permute-start
  72.9 12.7 collective-permute-start
  104.6 8.2 collective-permute-start
  118.4 7.1 collective-permute-start.3
  134.5 8.2 collective-permute-start
  148.3 6.9 collective-permute-start.3
  164.3 8.0 collective-permute-start
  177.9 5.9 collective-permute-start.3
  192.8 8.9 collective-permute-start
  207.4 6.7 collective-permute-start.3
  223.1 8.6 collective-permute-start
  237.3 6.1 collective-permute-start.3
  252.5 9.4 collective-permute-start
  267.4 7.0 collective-permute-start.3
  283.5 10.1 collective-permute-start
  299.4 6.7 collective-permute-start.3
  315.1 10.7 collective-permute-start
  331.4 5.8 collective-permute-start.3
  346.2 8.2 collective-permute-start
  360.0 6.3 collective-permute-start.3
  375.4 8.7 collective-permute-start
  389.7 6.8 collective-permute-start.3
  405.5 8.9 collective-permute-start
  420.1 7.4 collective-permute-start.3
  436.5 8.6 collective-permute-start
  450.7 6.9 collective-permute-start.3
  466.7 10.0 collective-permute-start
  497.7 143.1 %all-reduce.18.cloned.1.call-done = f32[2,2,2,6,512]{4,3,1,0,2:T(8,128)} async-done(((f32[2,2,2,6,512]{4,3,1,0,2:T(8,128)}), f32[2,2,2,6,512]{4,3,1,0,2:T(8,128)}) %all-reduce.18.cloned.1.call-update) | async-done | bytes 98320 | tf_op jit(solution)/shard_map/psum | solution.py:30
  653.4 716.9 %all-reduce.20.cloned.1.call-done = f32[384,2,2,2,64]{4,3,2,1,0:T(2,128)} async-done(((f32[384,2,2,2,64]{4,3,2,1,0:T(2,128)}), f32[384,2,2,2,64]{4,3,2,1,0:T(2,128)}) %all-reduce.20.cloned.1.call-update) | async-done | bytes 786448
  (683 shorter events, 262.1 us)
Async XLA Ops:
  7.2 633.7 %all-reduce.18.cloned.1.call-start = ((), (), s32[]{:S(2)}) async-start(), calls=%async_computation | async-start | bytes 262144 | tf_op jit(solution)/shard_map/psum | solution.py:30
  19.3 10.2 collective-permute-start.1
  45.5 9.3 collective-permute-start
  72.9 14.4 %collective-permute-start = (f32[6,6,1,512]{3,1,2,0:T(8,128)S(1)}, f32[6,6,1,512]{3,1,2,0:T(8,128)S(1)}, u32[]{:S(2)}, u32[]{:S(2)}) collective-permute-start(f32[6,6,1,512]{3,1,2,0:T(8,128)S(1)} %get-tuple-element.301), channel_id=1, source_target_pairs={{0,64},{64,128},{128,192},{192,256},{256,320},{320,384},{384,448},... | collective-permute-start | bytes 221192 | tf_op jit(solution)/shard_map/while/body/eval_jaxpr/ppermute | solution.py:20
  104.6 9.9 collective-permute-start
  116.4 10.0 collective-permute-start.2
  118.4 9.6 collective-permute-start.3
  134.5 9.9 collective-permute-start
  146.4 9.8 collective-permute-start.2
  148.3 9.3 collective-permute-start.3
  164.3 9.7 collective-permute-start
  192.8 10.6 collective-permute-start
  205.4 9.6 collective-permute-start.2
  223.1 10.3 collective-permute-start
  252.5 11.1 collective-permute-start
  265.5 9.9 collective-permute-start.2
  267.4 9.5 collective-permute-start.3
  283.5 11.8 collective-permute-start
  297.5 9.5 collective-permute-start.2
  315.1 12.4 collective-permute-start
  346.2 9.9 collective-permute-start
  375.4 10.4 collective-permute-start
  387.8 9.6 collective-permute-start.2
  389.7 9.2 collective-permute-start.3
  405.5 10.6 collective-permute-start
  418.1 10.3 collective-permute-start.2
  420.1 9.9 collective-permute-start.3
  436.5 10.3 collective-permute-start
  448.8 9.8 collective-permute-start.2
  450.7 9.4 collective-permute-start.3
  466.7 11.7 collective-permute-start
  496.4 873.9 %all-reduce.20.cloned.1.call-start = ((), (), s32[]{:S(2)}) async-start(), calls=%async_computation.1 | async-start | bytes 3145728
  (53 other events, 221.3 us)
Sparse Core Ops, SparseCore 0:
  496.5 144.3 all-reduce.17
  650.4 719.8 all-reduce.19
where the time goes:
time: 1380 us
  waiting for transfers between devices  924 us (67%)
  starting transfers between devices  287 us (21%)
  local copies, waits for them, and re-layouts  81.5 us (6%)
  other arithmetic  52.3 us (4%)
  between operations  14.9 us (1%)
    unnamed x3, waiting for transfers between devices  717 us
    ppermute x32, starting transfers between devices, padded_2(): lax.ppermute(lax.slice_in_dim(block, block.shape[dim] - width, None, axis...  235 us
    psum x1, waiting for transfers between devices, from_root(): return lax.psum(block, axis)  143 us
    ppermute x32, starting transfers between devices, padded_2(): lax.ppermute(lax.slice_in_dim(block, 0, width, axis=dim), axis, backward)  51.8 us
    another operation x112, local copies, waits for them, and re-layouts, yee_step(): return jnp.stack([new_x, new_y, new_z, magn_x, magn_y, magn_z])  40.2 us
    ppermute x32, waiting for transfers between devices, padded_2(): lax.ppermute(lax.slice_in_dim(block, 0, width, axis=dim), axis, backward)  38.8 us
  transfers between devices with their start and end apart: 66, of which 50 were waited for; matrix products, arithmetic and copies ran while one was open for 1% of the time, Pallas kernels for 0%

commit v1 on v0

--- a/solution.py
+++ b/solution.py
@@ -27,7 +27,7 @@
 
 def from_root(block, axis, owner):
     block = jnp.where(lax.axis_index(axis) == owner, block, jnp.zeros_like(block))
-    return lax.psum(block, axis)
+    return jnp.sum(lax.all_gather(block, axis), axis=0)
 
 
 def forward_diff(field, along):

time: 1380 us -> 1310 us (0.949)
  waiting for transfers between devices: 924 us -> 824 us
  blocking collectives: 0 us -> 30.8 us
    psum x1 -> x0, waiting for transfers between devices: 143 us -> none  [from_root(): return lax.psum(block, axis)]
    unnamed x3 -> x2, waiting for transfers between devices: 717 us -> 759 us
    all_gather x0 -> x1, blocking collectives: none -> 30.8 us  [from_root(): return jnp.sum(lax.all_gather(block, axis), axis=0)]
  transfers between devices with their start and end apart: 66 -> 65, of which waited for: 50 -> 49; matrix products, arithmetic and copies ran while one was open for 1% -> 1% of each run, Pallas kernels for 0% -> 0%
where the time goes in v1:
time: 1310 us
  waiting for transfers between devices  824 us (63%)
  starting transfers between devices  287 us (22%)
  local copies, waits for them, and re-layouts  81.6 us (6%)
  other arithmetic  53.1 us (4%)
  blocking collectives  30.8 us (2%)
  between operations  14.9 us (1%)
    unnamed x2, waiting for transfers between devices  759 us
    ppermute x32, starting transfers between devices, padded_2(): lax.ppermute(lax.slice_in_dim(block, block.shape[dim] - width, None, axis...  235 us
    ppermute x32, starting transfers between devices, padded_2(): lax.ppermute(lax.slice_in_dim(block, 0, width, axis=dim), axis, backward)  51.8 us
    another operation x112, local copies, waits for them, and re-layouts, yee_step(): return jnp.stack([new_x, new_y, new_z, magn_x, magn_y, magn_z])  40.2 us
    ppermute x32, waiting for transfers between devices, padded_2(): lax.ppermute(lax.slice_in_dim(block, 0, width, axis=dim), axis, backward)  38.7 us
    all_gather x1, blocking collectives, from_root(): return jnp.sum(lax.all_gather(block, axis), axis=0)  30.8 us
  transfers between devices with their start and end apart: 65, of which 49 were waited for; matrix products, arithmetic and copies ran while one was open for 1% of the time, Pallas kernels for 0%

profile of v1, /device:TPU:8, one launch (start us, length us, event | category | flops | bytes accessed | tf_op | source)
XLA Modules:
  0.0 1306.0 jit_solution(12515792505660795563)
XLA Ops:
  19.2 478.5 %while.16 = (s32[]{:T(128)}, f32[6,6,8,512]{3,0,1,2:T(8,128)S(1)}, f32[2,2,2,6,512]{4,3,2,1,0:T(8,128)S(1)}, f32[8,10,512]{2,0,1:T(8,128)S(1)}, f32[8,10,512]{2,...) while((s32[]{:T(128)}, f32[6,6,8,512]{3,0,1,2:T(8,128)S(1)}, ...), condition=%wide.region_1.2_spmd.clone, body=%wide.region_0.1_spmd.clone.sunk | while | flops 2527413 | bytes 23437268 | solution.py:160
  23.4 8.1 collective-permute-done.1
  47.5 7.6 collective-permute-start
  74.9 12.7 collective-permute-start
  106.6 8.2 collective-permute-start
  120.4 7.1 collective-permute-start.3
  136.6 8.2 collective-permute-start
  150.4 6.9 collective-permute-start.3
  166.4 8.0 collective-permute-start
  179.9 5.9 collective-permute-start.3
  194.9 8.9 collective-permute-start
  209.4 6.7 collective-permute-start.3
  225.2 8.6 collective-permute-start
  239.4 6.1 collective-permute-start.3
  254.5 9.4 collective-permute-start
  269.5 7.0 collective-permute-start.3
  285.6 10.1 collective-permute-start
  301.5 6.7 collective-permute-start.3
  317.2 10.7 collective-permute-start
  333.5 5.8 collective-permute-start.3
  348.3 8.2 collective-permute-start
  362.1 9.4 collective-permute-start.3
  380.6 8.7 collective-permute-start
  395.0 5.8 collective-permute-start.3
  409.8 8.2 collective-permute-start
  423.6 7.2 collective-permute-start.3
  439.8 8.4 collective-permute-start
  453.8 5.9 collective-permute-start.3
  468.7 9.0 collective-permute-start
  483.3 5.8 collective-permute-start.3
  497.9 30.8 %all-gather = f32[16,2,2,6,512]{4,2,3,1,0:T(2,128)S(1)} all-gather(f32[2,2,2,6,512]{4,2,3,1,0:T(2,128)S(1)} %copy_select_fusion), channel_id=2, replica_groups=mesh['depth'=8,'lat'=64] {'depth'}, dimensions={0}, use_global_device_ids=true | all-gather | bytes 884736 | tf_op jit(solution)/shard_map/all_gather | solution.py:30
  538.5 759.4 %all-reduce.17.cloned.1.call-done = f32[384,2,2,2,64]{4,3,2,1,0:T(2,128)} async-done(((f32[384,2,2,2,64]{4,3,2,1,0:T(2,128)}), f32[384,2,2,2,64]{4,3,2,1,0:T(2,128)}) %all-reduce.17.cloned.1.call-update) | async-done | bytes 786448
  (691 shorter events, 260.0 us)
Async XLA Ops:
  7.2 1290.6 %all-reduce.17.cloned.1.call-start = ((), (), s32[]{:S(2)}) async-start(), calls=%async_computation | async-start | bytes 3145728
  21.3 10.2 collective-permute-start.1
  47.5 9.3 collective-permute-start
  74.9 14.4 %collective-permute-start = (f32[6,6,1,512]{3,1,2,0:T(8,128)S(1)}, f32[6,6,1,512]{3,1,2,0:T(8,128)S(1)}, u32[]{:S(2)}, u32[]{:S(2)}) collective-permute-start(f32[6,6,1,512]{3,1,2,0:T(8,128)S(1)} %get-tuple-element.303), channel_id=1, source_target_pairs={{0,64},{64,128},{128,192},{192,256},{256,320},{320,384},{384,448},... | collective-permute-start | bytes 221192 | tf_op jit(solution)/shard_map/while/body/eval_jaxpr/ppermute | solution.py:20
  106.6 9.9 collective-permute-start
  118.5 10.0 collective-permute-start.2
  120.4 9.6 collective-permute-start.3
  136.6 9.9 collective-permute-start
  148.5 9.8 collective-permute-start.2
  150.4 9.3 collective-permute-start.3
  166.4 9.7 collective-permute-start
  194.9 10.6 collective-permute-start
  207.5 9.6 collective-permute-start.2
  209.4 9.2 collective-permute-start.3
  225.2 10.3 collective-permute-start
  237.4 8.9 collective-permute-start.2
  254.5 11.1 collective-permute-start
  267.6 9.9 collective-permute-start.2
  269.5 9.5 collective-permute-start.3
  285.6 11.8 collective-permute-start
  299.5 9.5 collective-permute-start.2
  301.5 9.1 collective-permute-start.3
  317.2 12.4 collective-permute-start
  348.3 9.9 collective-permute-start
  360.2 12.3 collective-permute-start.2
  362.1 11.9 collective-permute-start.3
  380.6 10.4 collective-permute-start
  409.8 9.9 collective-permute-start
  421.7 10.0 collective-permute-start.2
  423.6 9.6 collective-permute-start.3
  439.8 10.1 collective-permute-start
  468.7 10.7 collective-permute-start
  (56 other events, 338.8 us)
Sparse Core Ops, SparseCore 0:
  535.5 762.2 all-reduce.16
